TPU v7x, 512 devices: a whole 4x8x8 slice. The times are simulated.
512 devices in a mesh: dp: 64 (over x, z, core), tensor: 8 (over y).
Axes of the slice: x: 4, y: 8, z: 8, core: 2. Of those that a mesh axis runs over, the one named last changes fastest.
Arguments:
- prompt_keys: bfloat16 [4096, 1024], P('dp', 'tensor'), may hold values from -6 to 6
- prompt_values: bfloat16 [4096, 1024], P('dp', 'tensor'), may hold values from -6 to 6
- key_weight: bfloat16 [5120, 1024], P('dp', 'tensor'), may hold values from -0.078125 to 0.078125
- value_weight: bfloat16 [5120, 1024], P('dp', 'tensor'), may hold values from -0.078125 to 0.078125
- resp_query: bfloat16 [8192, 8192], P('dp', 'tensor'), may hold values from -6 to 6
- resp_keys: bfloat16 [8192, 1024], P('dp', 'tensor'), may hold values from -6 to 6
- resp_values: bfloat16 [8192, 1024], P('dp', 'tensor'), may hold values from -6 to 6
- resp_grad: bfloat16 [8192, 8192], P('dp', 'tensor'), may hold values from -48 to 48
- resp_lse: float32 [64, 8192], P('tensor', 'dp'), as said below
- resp_delta: float32 [64, 8192], P('tensor', 'dp'), may hold values from -24 to 24
- resp_prompt: int32 [1024], replicated, may hold values from 0 to 63, as said below
- resp_lengths: int32 [1024], P('dp'), may hold values from 1 to 8, 5120 in all
Outputs:
- d_query: bfloat16 [8192, 8192], P('dp', 'tensor')
- d_resp_keys: bfloat16 [8192, 1024], P('dp', 'tensor')
- d_resp_values: bfloat16 [8192, 1024], P('dp', 'tensor')
- d_prompt_input: bfloat16 [4096, 5120], P('dp', 'tensor')
Inputs may be any that keep to these rules, and one draw needn't show every extreme that they name: `resp_prompt`: response r sits on index r // 16 of dp, in slot r % 16, and prompt p on index p. For each slot number s, the responses in slot s of all indices of dp name every prompt exactly once; so each prompt is named by exactly 16 responses, and the 16 responses of one index of dp name 16 different prompts. `resp_lse`: within 0.5 below and 1.5 above log(72).
All inputs are finite; a program needn't handle non-finite values. No bound on the sum of `resp_lengths` on one device may be relied on, other than what follows from the above.
Results may differ from a plain program's by a relative error of at most 0.006.
Values may be sent and summed in bfloat16 or wider, within the bound.
A program may use at most 64 MiB of HBM per device.

v0:
```python
import jax
import jax.numpy as jnp
from jax import lax
from jax.sharding import PartitionSpec as P

QH = 64
KVH = 8
HD = 128


def attend_back(query, grad_live, log_norm, row_delta, key_rows, value_rows, key_mask):
    scaling = query.shape[-1] ** (-0.5)
    scores = (
        jnp.einsum("crlgqd,cmgd->crlgqm", query, key_rows, preferred_element_type=jnp.float32)
        * scaling
    )
    probs = jnp.exp(scores - log_norm[..., None])
    if key_mask is not None:
        probs = jnp.where(key_mask[:, None, None, :], probs, jnp.float32(0.0))
    probs_low = probs.astype(jnp.bfloat16)
    dprob = jnp.einsum(
        "crlgqd,cmgd->crlgqm", grad_live, value_rows, preferred_element_type=jnp.float32
    )
    dscore = (probs * (dprob - row_delta[..., None])).astype(jnp.bfloat16)
    grad_values = jnp.einsum(
        "crlgqm,crlgqd->cmgd", probs_low, grad_live, preferred_element_type=jnp.float32
    )
    grad_keys = (
        jnp.einsum("crlgqm,crlgqd->cmgd", dscore, query, preferred_element_type=jnp.float32)
        * scaling
    )
    grad_query = (
        jnp.einsum("crlgqm,cmgd->crlgqd", dscore, key_rows, preferred_element_type=jnp.float32)
        * scaling
    )
    return (grad_query, grad_keys, grad_values)


def prefix_scan(items, own_keys, own_values, group_size):
    count = items[0].shape[0]
    blocks = tuple(
        (
            part_array.reshape((count // group_size, group_size) + part_array.shape[1:])
            for part_array in items
        )
    )
    kv_local = own_keys.shape[2]
    head_size = own_keys.shape[3]

    def one_block(carry, block):
        got_query, got_grad, got_norm, got_delta = block
        rows_n, rows_l = (got_query.shape[0], got_query.shape[1])
        shaped_query = got_query.reshape(1, rows_n, rows_l, kv_local, -1, head_size)
        shaped_grad = got_grad.reshape(1, rows_n, rows_l, kv_local, -1, head_size)
        grad_query, grad_keys, grad_values = attend_back(
            shaped_query, shaped_grad, got_norm[None], got_delta[None], own_keys, own_values, None
        )
        return (
            (carry[0] + grad_keys, carry[1] + grad_values),
            grad_query.reshape(rows_n, rows_l, -1),
        )

    start_sums = (jnp.zeros(own_keys.shape, jnp.float32), jnp.zeros(own_keys.shape, jnp.float32))
    (key_sum, value_sum), block_dq = lax.scan(one_block, start_sums, blocks)
    return (key_sum, value_sum, block_dq.reshape((count,) + block_dq.shape[2:]))


def contract(left, right):
    return lax.dot_general(
        left, right, (((1,), (1,)), ((), ())), preferred_element_type=jnp.float32
    )


def body(
    prompt_keys,
    prompt_values,
    key_weight,
    value_weight,
    resp_query,
    resp_keys,
    resp_values,
    resp_grad,
    resp_lse,
    resp_delta,
    resp_prompt,
    resp_lengths,
):
    dev_count = lax.axis_size("dp")
    my_index = lax.axis_index("dp")
    group_heads = QH // KVH
    kv_local = resp_keys.shape[1] // HD
    slots = resp_lengths.shape[0]
    resp_len = resp_query.shape[0] // slots
    prompt_len = prompt_keys.shape[0]
    feat_width = resp_query.shape[1]
    zero_low = jnp.zeros((), jnp.bfloat16)
    shaped = (slots, resp_len, kv_local, group_heads, HD)
    valid = jnp.arange(resp_len)[None, :] < resp_lengths[:, None]
    query = resp_query.reshape(shaped)
    grad_live = jnp.where(valid[:, :, None, None, None], resp_grad.reshape(shaped), zero_low)
    log_norm = resp_lse.reshape(kv_local, group_heads, slots, resp_len).transpose(2, 3, 0, 1)
    delta_all = resp_delta.reshape(kv_local, group_heads, slots, resp_len).transpose(2, 3, 0, 1)
    delta_live = jnp.where(valid[:, :, None, None], delta_all, jnp.float32(0.0))
    placed = resp_prompt.reshape(dev_count, slots)
    my_prompts = lax.dynamic_slice_in_dim(placed, my_index, 1, 0)[0]
    flat_query = resp_query.reshape(slots, resp_len, feat_width)
    flat_grad = grad_live.reshape(slots, resp_len, feat_width)
    causal = jnp.arange(resp_len)[:, None] >= jnp.arange(resp_len)[None, :]
    key_local = resp_keys.reshape(slots, resp_len, kv_local, HD)
    value_local = resp_values.reshape(slots, resp_len, kv_local, HD)
    local_dq, local_dk, local_dv = attend_back(
        query[:, None],
        grad_live[:, None],
        log_norm[:, None],
        delta_live[:, None],
        key_local,
        value_local,
        causal,
    )
    d_resp_keys = local_dk.astype(jnp.bfloat16).reshape(slots * resp_len, kv_local * HD)
    d_resp_values = local_dv.astype(jnp.bfloat16).reshape(slots * resp_len, kv_local * HD)
    own_keys = prompt_keys.reshape(1, prompt_len, kv_local, HD)
    own_values = prompt_values.reshape(1, prompt_len, kv_local, HD)
    match = my_prompts[None, :] == jnp.arange(dev_count)[:, None]
    present = jnp.any(match, axis=1)
    dest_slot = jnp.sum(jnp.where(match, jnp.arange(slots)[None, :], 0), axis=1)
    send_query = jnp.where(
        present[:, None, None], jnp.take(flat_query, dest_slot, axis=0), zero_low
    )
    send_grad = jnp.where(present[:, None, None], jnp.take(flat_grad, dest_slot, axis=0), zero_low)
    send_norm = jnp.where(
        present[:, None, None, None], jnp.take(log_norm, dest_slot, axis=0), jnp.float32(0.0)
    )
    send_delta = jnp.where(
        present[:, None, None, None], jnp.take(delta_live, dest_slot, axis=0), jnp.float32(0.0)
    )
    send_query, send_grad, send_norm, send_delta = (send_query, send_grad, send_norm, send_delta)
    got_query, got_grad = (
        lax.all_to_all(send_query, "dp", split_axis=0, concat_axis=0, tiled=True),
        lax.all_to_all(send_grad, "dp", split_axis=0, concat_axis=0, tiled=True),
    )
    got_norm, got_delta = (
        lax.all_to_all(send_norm, "dp", split_axis=0, concat_axis=0, tiled=True),
        lax.all_to_all(send_delta, "dp", split_axis=0, concat_axis=0, tiled=True),
    )
    key_sum, value_sum, block_dq = prefix_scan(
        (got_query, got_grad, got_norm, got_delta), own_keys, own_values, slots
    )
    prefix_dq = block_dq.astype(jnp.bfloat16)
    returned = lax.all_to_all(prefix_dq, "dp", split_axis=0, concat_axis=0, tiled=True)
    mine = jnp.take(returned, my_prompts, axis=0)
    d_query = (local_dq.reshape(slots, resp_len, feat_width) + mine.astype(jnp.float32)).astype(
        jnp.bfloat16
    )
    d_query = d_query.reshape(slots * resp_len, feat_width)
    dk_low = key_sum.reshape(prompt_len, kv_local * HD).astype(jnp.bfloat16)
    dv_low = value_sum.reshape(prompt_len, kv_local * HD).astype(jnp.bfloat16)
    stacked = jnp.stack((key_weight, value_weight))
    piece = lax.all_gather(stacked, "dp", axis=1, tiled=True)
    partial_sum = contract(dk_low, piece[0]) + contract(dv_low, piece[1])
    summed = lax.psum_scatter(partial_sum, "tensor", scatter_dimension=1, tiled=True)
    d_prompt_input = summed.astype(jnp.bfloat16)
    return (d_query, d_resp_keys, d_resp_values, d_prompt_input)


def solution(mesh):
    placed = (
        P("dp", "tensor"),
        P("dp", "tensor"),
        P("dp", "tensor"),
        P("dp", "tensor"),
        P("dp", "tensor"),
        P("dp", "tensor"),
        P("dp", "tensor"),
        P("dp", "tensor"),
        P("tensor", "dp"),
        P("tensor", "dp"),
        P(),
        P("dp"),
    )
    return jax.shard_map(
        body,
        mesh=mesh,
        in_specs=placed,
        out_specs=(P("dp", "tensor"), P("dp", "tensor"), P("dp", "tensor"), P("dp", "tensor")),
        check_vma=False,
    )
```

profile of v0, /device:TPU:2, one launch (start us, length us, event | category | flops | bytes accessed | tf_op | source)
XLA Modules:
  0.0 240.0 jit_solution(2691822412907780129)
XLA Ops:
  7.2 0.8 reshape.275
  8.2 0.4 copy-done.7
  8.6 0.8 copy.93
  9.4 0.8 copy.94
  10.2 0.7 iota_compare_fusion.1
  11.0 0.6 gather_fusion.4
  11.7 0.6 gather_fusion.2
  12.3 1.0 fusion.39
  13.3 13.9 %all-to-all-start.1 = ((f32[64,8,1,8]{3,1,2,0:T(8,128)}), f32[64,8,1,8]{3,1,2,0:T(8,128)S(1)}, u32[]{:S(2)}, u32[]{:S(2)}) async-start(f32[64,8,1,8]{3,1,2,0:T(8,128)} %get-tuple-element.163), calls=%async_computation.1 | async-start | bytes 524288 | tf_op jit(solution)/shard_map/all_to_all | solution.py:143
  27.3 0.6 gather_fusion.3
  27.9 0.6 gather_fusion.1
  28.5 10.2 %all-to-all-done.1 = f32[64,8,1,8]{3,1,2,0:T(8,128)S(1)} async-done(((f32[64,8,1,8]{3,1,2,0:T(8,128)}), f32[64,8,1,8]{3,1,2,0:T(8,128)S(1)}, u32[]{:S(2)}, u32[]{:S(2)}) %all-to-all-start.1) | async-done | bytes 16416 | tf_op jit(solution)/shard_map/all_to_all | solution.py:143
  38.7 0.7 copy-done.4
  39.4 6.7 %all-to-all-start.3 = ((f32[64,8,1,8]{3,1,2,0:T(8,128)}), f32[64,8,1,8]{3,1,2,0:T(8,128)}, u32[]{:S(2)}, u32[]{:S(2)}) async-start(f32[64,8,1,8]{3,1,2,0:T(8,128)} %get-tuple-element.162), calls=%async_computation.3 | async-start | bytes 524288 | tf_op jit(solution)/shard_map/all_to_all | solution.py:144
  46.1 1.3 select_select_fusion
  47.4 10.1 %all-to-all-done.3 = f32[64,8,1,8]{3,1,2,0:T(8,128)} async-done(((f32[64,8,1,8]{3,1,2,0:T(8,128)}), f32[64,8,1,8]{3,1,2,0:T(8,128)}, u32[]{:S(2)}, u32[]{:S(2)}) %all-to-all-start.3) | async-done | bytes 16416 | tf_op jit(solution)/shard_map/all_to_all | solution.py:144
  57.5 33.4 %all_to_all.25 = bf16[64,8,1024]{2,1,0:T(8,128)(2,1)S(1)} all-to-all(bf16[64,8,1024]{2,1,0:T(8,128)(2,1)S(1)} %get-tuple-element.165), channel_id=1, replica_groups=mesh['dp'=64,'tensor'=8] {'dp'}, dimensions={0} | all-to-all | bytes 2097152 | tf_op jit(solution)/shard_map/all_to_all | solution.py:139
  91.0 8.0 %all-to-all-start.2 = ((bf16[64,8,1024]{2,1,0:T(8,128)(2,1)}), bf16[64,8,1024]{2,1,0:T(8,128)(2,1)}, u32[]{:S(2)}, u32[]{:S(2)}) async-start(bf16[64,8,1024]{2,1,0:T(8,128)(2,1)} %get-tuple-element.164), calls=%async_computation.2 | async-start | bytes 2097152 | tf_op jit(solution)/shard_map/all_to_all | solution.py:140
  99.0 0.6 pad_maximum_fusion
  99.7 26.2 %all-to-all-done.2 = bf16[64,8,1024]{2,1,0:T(8,128)(2,1)} async-done(((bf16[64,8,1024]{2,1,0:T(8,128)(2,1)}), bf16[64,8,1024]{2,1,0:T(8,128)(2,1)}, u32[]{:S(2)}, u32[]{:S(2)}) %all-to-all-start.2) | async-done | bytes 1048608 | tf_op jit(solution)/shard_map/all_to_all | solution.py:140
  126.0 15.7 %while.15 = (s32[]{:T(128)}, f32[1,64,1,128]{3,1,2,0:T(8,128)S(1)}, f32[1,64,1,128]{3,1,2,0:T(8,128)S(1)}, bf16[4,16,8,1024]{3,2,1,0:T(8,128)(2,1)}, bf16[4,16,8...) while((s32[]{:T(128)}, f32[1,64,1,128]{3,1,2,0:T(8,128)S(1)}, ...), condition=%wide.region_3.6_spmd.clone, body=%wide.region_2.5_spmd.clone.sunk | while | flops 84582400 | bytes 4792468 | solution.py:64
  126.0 0.9 dynamic-slice_bitcast_fusion.6
  126.8 1.0 dynamic-slice_bitcast_fusion.7
  127.8 0.2 fusion.85
  128.1 0.2 fusion.86
  128.3 0.2 fusion.87
  128.6 0.2 fusion.88
  129.2 0.7 constant_dynamic-update-slice_fusion.2
  129.9 0.9 dynamic-slice_bitcast_fusion.6
  130.8 1.0 dynamic-slice_bitcast_fusion.7
  131.8 0.2 fusion.85
  132.0 0.2 fusion.86
  132.3 0.2 fusion.87
  132.5 0.2 fusion.88
  133.1 0.7 constant_dynamic-update-slice_fusion.2
  133.8 0.9 dynamic-slice_bitcast_fusion.6
  134.7 1.0 dynamic-slice_bitcast_fusion.7
  135.7 0.2 fusion.85
  136.0 0.2 fusion.86
  136.2 0.2 fusion.87
  136.5 0.2 fusion.88
  137.0 0.7 constant_dynamic-update-slice_fusion.2
  137.8 0.9 dynamic-slice_bitcast_fusion.6
  138.7 1.0 dynamic-slice_bitcast_fusion.7
  139.6 0.2 fusion.85
  139.9 0.2 fusion.86
  140.2 0.2 fusion.87
  140.4 0.2 fusion.88
  141.0 0.7 constant_dynamic-update-slice_fusion.2
  141.7 46.2 %all-gather.2.cloned.1.call-done = bf16[2,5120,128]{2,1,0:T(8,128)(2,1)} async-done(((bf16[2,80,128]{2,1,0:T(8,128)(2,1)}), bf16[2,5120,128]{2,1,0:T(8,128)(2,1)}) %all-gather.2.cloned.1.call-update) | async-done | bytes 2621456 | tf_op jit(solution)/shard_map/all_gather | solution.py:159
  187.9 2.0 fusion.19
  190.1 1.6 convolution_add_fusion
  191.8 7.6 %all-to-all-start.4 = ((bf16[64,8,1024]{2,1,0:T(8,128)(2,1)}), bf16[64,8,1024]{2,1,0:T(8,128)(2,1)S(1)}, u32[]{:S(2)}, u32[]{:S(2)}) async-start(bf16[64,8,1024]{2,1,0:T(8,128)(2,1)} %bitcast.41), calls=%async_computation.4 | async-start | bytes 2097152 | tf_op jit(solution)/shard_map/all_to_all | solution.py:150
  199.6 0.7 fusion.56
  200.3 1.3 fusion.28
  201.6 1.3 fusion.30
  203.0 1.0 fusion.34
  204.0 1.0 fusion.35
  205.0 0.3 fusion.20
  205.3 21.3 %all-to-all-done.4 = bf16[64,8,1024]{2,1,0:T(8,128)(2,1)S(1)} async-done(((bf16[64,8,1024]{2,1,0:T(8,128)(2,1)}), bf16[64,8,1024]{2,1,0:T(8,128)(2,1)S(1)}, u32[]{:S(2)}, u32[]{:S(2)}) %all-to-all-start.4) | async-done | bytes 1048608 | tf_op jit(solution)/shard_map/all_to_all | solution.py:150
  226.6 0.6 gather_fusion
  227.1 0.9 fusion.36
  228.0 3.5 %reduce-scatter.2.cloned.1.call-done = f32[64,640]{1,0:T(8,128)} async-done(((f32[64,5120]{1,0:T(8,128)}), f32[64,640]{1,0:T(8,128)}) %reduce-scatter.2.cloned.1.call-update) | async-done | bytes 163856 | tf_op jit(solution)/shard_map/reduce_scatter | solution.py:161
  231.6 1.6 convert_element_type.80
  (49 shorter events, 2.2 us)
Async XLA Ops:
  7.2 20.7 %copy-start = (bf16[128,1024]{1,0:T(8,128)(2,1)S(1)}, bf16[128,1024]{1,0:T(8,128)(2,1)}, u32[]{:S(2)}) copy-start(bf16[128,1024]{1,0:T(8,128)(2,1)} %param.22) | copy-start | bytes 786436
  8.0 0.6 copy-start.7
  11.0 16.2 %copy-start.2 = (bf16[128,1024]{1,0:T(8,128)(2,1)S(1)}, bf16[128,1024]{1,0:T(8,128)(2,1)}, u32[]{:S(2)}) copy-start(bf16[128,1024]{1,0:T(8,128)(2,1)} %param.25) | copy-start | bytes 786436
  13.3 25.4 %all-to-all-start.1 = ((f32[64,8,1,8]{3,1,2,0:T(8,128)}), f32[64,8,1,8]{3,1,2,0:T(8,128)S(1)}, u32[]{:S(2)}, u32[]{:S(2)}) async-start(f32[64,8,1,8]{3,1,2,0:T(8,128)} %get-tuple-element.163), calls=%async_computation.1 | async-start | bytes 524288 | tf_op jit(solution)/shard_map/all_to_all | solution.py:143
  38.7 0.7 copy-start.4
  39.4 18.1 %all-to-all-start.3 = ((f32[64,8,1,8]{3,1,2,0:T(8,128)}), f32[64,8,1,8]{3,1,2,0:T(8,128)}, u32[]{:S(2)}, u32[]{:S(2)}) async-start(f32[64,8,1,8]{3,1,2,0:T(8,128)} %get-tuple-element.162), calls=%async_computation.3 | async-start | bytes 524288 | tf_op jit(solution)/shard_map/all_to_all | solution.py:144
  90.9 8.0 %copy-start.10 = (bf16[80,128]{1,0:T(8,128)(2,1)S(1)}, bf16[80,128]{1,0:T(8,128)(2,1)}, u32[]{:S(2)}) copy-start(bf16[80,128]{1,0:T(8,128)(2,1)} %param.21) | copy-start | bytes 61444
  90.9 8.0 %copy-start.11 = (bf16[80,128]{1,0:T(8,128)(2,1)S(1)}, bf16[80,128]{1,0:T(8,128)(2,1)}, u32[]{:S(2)}) copy-start(bf16[80,128]{1,0:T(8,128)(2,1)} %param.20) | copy-start | bytes 61444
  90.9 35.0 %copy-start.5 = (bf16[64,128]{1,0:T(8,128)(2,1)S(1)}, bf16[64,128]{1,0:T(8,128)(2,1)}, u32[]{:S(2)}) copy-start(bf16[64,128]{1,0:T(8,128)(2,1)} %param.19) | copy-start | bytes 49156
  90.9 35.0 %copy-start.6 = (bf16[64,128]{1,0:T(8,128)(2,1)S(1)}, bf16[64,128]{1,0:T(8,128)(2,1)}, u32[]{:S(2)}) copy-start(bf16[64,128]{1,0:T(8,128)(2,1)} %param.18) | copy-start | bytes 49156
  91.0 35.0 %all-to-all-start.2 = ((bf16[64,8,1024]{2,1,0:T(8,128)(2,1)}), bf16[64,8,1024]{2,1,0:T(8,128)(2,1)}, u32[]{:S(2)}, u32[]{:S(2)}) async-start(bf16[64,8,1024]{2,1,0:T(8,128)(2,1)} %get-tuple-element.164), calls=%async_computation.2 | async-start | bytes 2097152 | tf_op jit(solution)/shard_map/all_to_all | solution.py:140
  98.9 89.0 %all-gather.2.cloned.1.call-start = ((), (), s32[]{:S(2)}) async-start(), calls=%async_computation.6 | async-start | bytes 2662400 | tf_op jit(solution)/shard_map/all_gather | solution.py:159
  99.7 131.9 %reduce-scatter.2.cloned.1.call-start = ((), (), s32[]{:S(2)}) async-start(), calls=%async_computation.7 | async-start | bytes 1474560 | tf_op jit(solution)/shard_map/reduce_scatter | solution.py:161
  187.9 2.1 copy-start.1
  191.8 8.6 %copy-start.9 = (bf16[128,128]{1,0:T(8,128)(2,1)S(1)}, bf16[128,128]{1,0:T(8,128)(2,1)}, u32[]{:S(2)}) copy-start(bf16[128,128]{1,0:T(8,128)(2,1)} %param.23) | copy-start | bytes 98308
  191.8 9.8 %copy-start.3 = (bf16[128,1024]{1,0:T(8,128)(2,1)S(1)}, bf16[128,1024]{1,0:T(8,128)(2,1)}, u32[]{:S(2)}) copy-start(bf16[128,1024]{1,0:T(8,128)(2,1)} %param.25) | copy-start | bytes 786436
  191.8 9.8 %copy-start.8 = (bf16[128,128]{1,0:T(8,128)(2,1)S(1)}, bf16[128,128]{1,0:T(8,128)(2,1)}, u32[]{:S(2)}) copy-start(bf16[128,128]{1,0:T(8,128)(2,1)} %param.24) | copy-start | bytes 98308
  191.8 34.8 %all-to-all-start.4 = ((bf16[64,8,1024]{2,1,0:T(8,128)(2,1)}), bf16[64,8,1024]{2,1,0:T(8,128)(2,1)S(1)}, u32[]{:S(2)}, u32[]{:S(2)}) async-start(bf16[64,8,1024]{2,1,0:T(8,128)(2,1)} %bitcast.41), calls=%async_computation.4 | async-start | bytes 2097152 | tf_op jit(solution)/shard_map/all_to_all | solution.py:150
Sparse Core Ops, SparseCore 0:
  103.6 84.2 all-gather.1
  191.9 39.6 reduce-scatter.1
where the time goes:
time: 241 us; the launch traced here: 240 us
  waiting for transfers between devices  118 us (49%)
  starting transfers between devices  36.2 us (15%)
  blocking collectives  33.4 us (14%)
  local copies, waits for them, and re-layouts  17.7 us (7%)
  between operations  14.3 us (6%)
  matrix products  13.3 us (6%)
  other arithmetic  7.21 us (3%)
    all_gather x1, waiting for transfers between devices, body(): piece = lax.all_gather(stacked, 'dp', axis=1, tiled=True)  46.2 us
    all_to_all x1, blocking collectives, body(): lax.all_to_all(send_query, 'dp', split_axis=0, concat_axis=0, tiled=True)  33.4 us
    all_to_all x1, waiting for transfers between devices, body(): lax.all_to_all(send_grad, 'dp', split_axis=0, concat_axis=0, tiled=True)  26.2 us
    all_to_all x1, waiting for transfers between devices, body(): lax.all_to_all(prefix_dq, 'dp', split_axis=0, concat_axis=0, tiled=True)  21.3 us
    all_to_all x1, starting transfers between devices, body(): lax.all_to_all(send_norm, 'dp', split_axis=0, concat_axis=0, tiled=True)  13.9 us
    all_to_all x1, waiting for transfers between devices, body(): lax.all_to_all(send_norm, 'dp', split_axis=0, concat_axis=0, tiled=True)  10.2 us
    all_to_all x1, waiting for transfers between devices, body(): lax.all_to_all(send_delta, 'dp', split_axis=0, concat_axis=0, tiled=True)  10.1 us
    all_to_all x1, starting transfers between devices, body(): lax.all_to_all(send_grad, 'dp', split_axis=0, concat_axis=0, tiled=True)  7.95 us
  transfers between devices with their start and end apart: 6, of which 6 were waited for; matrix products, arithmetic and copies ran while one was open for 11% of the time, Pallas kernels for 0%

commit v1 on v0

--- a/solution.py
+++ b/solution.py
@@ -156,7 +156,9 @@
     dk_low = key_sum.reshape(prompt_len, kv_local * HD).astype(jnp.bfloat16)
     dv_low = value_sum.reshape(prompt_len, kv_local * HD).astype(jnp.bfloat16)
     stacked = jnp.stack((key_weight, value_weight))
-    piece = lax.all_gather(stacked, "dp", axis=1, tiled=True)
+    piece = jnp.concatenate(
+        lax.all_to_all(jnp.stack([stacked] * lax.axis_size("dp")), "dp", 0, 0), axis=1
+    )
     partial_sum = contract(dk_low, piece[0]) + contract(dv_low, piece[1])
     summed = lax.psum_scatter(partial_sum, "tensor", scatter_dimension=1, tiled=True)
     d_prompt_input = summed.astype(jnp.bfloat16)

time: 241 us -> 250 us (1.037)
  the two profiles are of different devices: /device:TPU:2 before, /device:TPU:4 now
where the time goes in v1:
time: 250 us; the launch traced here: 248 us
  waiting for transfers between devices  99.9 us (40%)
  starting transfers between devices  46.2 us (18%)
  blocking collectives  33 us (13%)
  matrix products  28.6 us (11%)
  local copies, waits for them, and re-layouts  18.9 us (8%)
  between operations  14.4 us (6%)
  other arithmetic  7.15 us (3%)
    all_to_all x1, blocking collectives, body(): lax.all_to_all(send_grad, 'dp', split_axis=0, concat_axis=0, tiled=True)  33 us
    all_to_all x1, waiting for transfers between devices, body(): lax.all_to_all(jnp.stack([stacked] * lax.axis_size('dp')), 'dp', 0, 0)  28 us
    all_to_all x1, waiting for transfers between devices, body(): lax.all_to_all(send_query, 'dp', split_axis=0, concat_axis=0, tiled=True)  26.6 us
    all_to_all x1, waiting for transfers between devices, body(): lax.all_to_all(prefix_dq, 'dp', split_axis=0, concat_axis=0, tiled=True)  20.8 us
    all_to_all x1, starting transfers between devices, body(): lax.all_to_all(send_delta, 'dp', split_axis=0, concat_axis=0, tiled=True)  14.1 us
    all_to_all x1, waiting for transfers between devices, body(): lax.all_to_all(send_norm, 'dp', split_axis=0, concat_axis=0, tiled=True)  10.2 us
    all_to_all x1, waiting for transfers between devices, body(): lax.all_to_all(send_delta, 'dp', split_axis=0, concat_axis=0, tiled=True)  10.1 us
    all_to_all x1, starting transfers between devices, body(): lax.all_to_all(prefix_dq, 'dp', split_axis=0, concat_axis=0, tiled=True)  8.91 us
  transfers between devices with their start and end apart: 6, of which 6 were waited for; matrix products, arithmetic and copies ran while one was open for 17% of the time, Pallas kernels for 0%

profile of v1, /device:TPU:4, one launch (start us, length us, event | category | flops | bytes accessed | tf_op | source)
XLA Modules:
  0.0 248.2 jit_solution(15018884568402957486)
XLA Ops:
  7.2 0.8 reshape.285
  8.0 0.6 compare_and_fusion.1
  8.8 0.7 iota_compare_fusion.1
  9.5 0.8 copy.93
  10.3 0.8 copy.94
  11.2 0.6 gather_fusion.4
  11.8 0.6 gather_fusion.2
  12.5 1.0 fusion.38
  13.5 14.1 %all-to-all-start.3 = ((f32[64,8,1,8]{3,1,2,0:T(8,128)}), f32[64,8,1,8]{3,1,2,0:T(8,128)}, u32[]{:S(2)}, u32[]{:S(2)}) async-start(f32[64,8,1,8]{3,1,2,0:T(8,128)} %get-tuple-element.164), calls=%async_computation.3 | async-start | bytes 524288 | tf_op jit(solution)/shard_map/all_to_all | solution.py:144
  27.7 0.6 gather_fusion.3
  28.3 0.6 gather_fusion.1
  29.0 10.1 %all-to-all-done.3 = f32[64,8,1,8]{3,1,2,0:T(8,128)} async-done(((f32[64,8,1,8]{3,1,2,0:T(8,128)}), f32[64,8,1,8]{3,1,2,0:T(8,128)}, u32[]{:S(2)}, u32[]{:S(2)}) %all-to-all-start.3) | async-done | bytes 16416 | tf_op jit(solution)/shard_map/all_to_all | solution.py:144
  39.1 6.7 %all-to-all-start.1 = ((f32[64,8,1,8]{3,1,2,0:T(8,128)}), f32[64,8,1,8]{3,1,2,0:T(8,128)}, u32[]{:S(2)}, u32[]{:S(2)}) async-start(f32[64,8,1,8]{3,1,2,0:T(8,128)} %get-tuple-element.165), calls=%async_computation.1 | async-start | bytes 524288 | tf_op jit(solution)/shard_map/all_to_all | solution.py:143
  45.7 1.3 select_select_fusion
  47.0 10.2 %all-to-all-done.1 = f32[64,8,1,8]{3,1,2,0:T(8,128)} async-done(((f32[64,8,1,8]{3,1,2,0:T(8,128)}), f32[64,8,1,8]{3,1,2,0:T(8,128)}, u32[]{:S(2)}, u32[]{:S(2)}) %all-to-all-start.1) | async-done | bytes 16416 | tf_op jit(solution)/shard_map/all_to_all | solution.py:143
  57.2 33.0 %all_to_all.30 = bf16[64,8,1024]{2,1,0:T(8,128)(2,1)} all-to-all(bf16[64,8,1024]{2,1,0:T(8,128)(2,1)S(1)} %get-tuple-element.166), channel_id=1, replica_groups=mesh['dp'=64,'tensor'=8] {'dp'}, dimensions={0} | all-to-all | bytes 2097152 | tf_op jit(solution)/shard_map/all_to_all | solution.py:140
  90.2 8.2 %all-to-all-start = ((bf16[64,8,1024]{2,1,0:T(8,128)(2,1)}), bf16[64,8,1024]{2,1,0:T(8,128)(2,1)S(1)}, u32[]{:S(2)}, u32[]{:S(2)}) async-start(bf16[64,8,1024]{2,1,0:T(8,128)(2,1)} %get-tuple-element.167), calls=%async_computation | async-start | bytes 2097152 | tf_op jit(solution)/shard_map/all_to_all | solution.py:139
  98.5 26.6 %all-to-all-done = bf16[64,8,1024]{2,1,0:T(8,128)(2,1)S(1)} async-done(((bf16[64,8,1024]{2,1,0:T(8,128)(2,1)}), bf16[64,8,1024]{2,1,0:T(8,128)(2,1)S(1)}, u32[]{:S(2)}, u32[]{:S(2)}) %all-to-all-start) | async-done | bytes 1048608 | tf_op jit(solution)/shard_map/all_to_all | solution.py:139
  125.1 1.8 stack.11
  127.0 8.2 %all-to-all-start.5 = ((bf16[64,2,80,128]{3,2,1,0:T(8,128)(2,1)}), bf16[64,2,80,128]{3,2,1,0:T(8,128)(2,1)S(1)}, u32[]{:S(2)}, u32[]{:S(2)}) async-start(bf16[64,2,80,128]{3,2,1,0:T(8,128)(2,1)} %stack.11), calls=%async_computation.5 | async-start | bytes 5242880 | tf_op jit(solution)/shard_map/all_to_all | solution.py:160
  135.3 31.3 %while.15 = (s32[]{:T(128)}, f32[1,64,1,128]{3,1,2,0:T(8,128)}, f32[1,64,1,128]{3,1,2,0:T(8,128)}, bf16[4,16,8,1024]{3,2,1,0:T(8,128)(2,1)}, bf16[4,16,8,1024]{3...) while((s32[]{:T(128)}, f32[1,64,1,128]{3,1,2,0:T(8,128)}, ...), condition=%wide.region_3.6_spmd.clone, body=%wide.region_2.5_spmd.clone.sunk | while | flops 84582400 | bytes 4792468 | solution.py:64
  135.3 0.9 dynamic-slice_bitcast_fusion.6
  136.2 1.1 dynamic-slice_bitcast_fusion.7
  137.2 1.0 fusion.88
  138.2 0.9 fusion.91
  139.3 0.9 fusion.90
  140.2 0.9 fusion.92
  141.2 0.7 constant_dynamic-update-slice_fusion.2
  141.9 0.9 dynamic-slice_bitcast_fusion.6
  142.8 1.1 dynamic-slice_bitcast_fusion.7
  143.9 1.0 fusion.88
  144.9 1.6 fusion.91
  146.7 1.6 fusion.90
  148.4 0.9 fusion.92
  149.4 0.7 constant_dynamic-update-slice_fusion.2
  150.2 0.9 dynamic-slice_bitcast_fusion.6
  151.0 1.1 dynamic-slice_bitcast_fusion.7
  152.1 1.0 fusion.88
  153.1 1.6 fusion.91
  154.9 1.6 fusion.90
  156.6 0.9 fusion.92
  157.6 0.7 constant_dynamic-update-slice_fusion.2
  158.3 0.9 dynamic-slice_bitcast_fusion.6
  159.2 1.1 dynamic-slice_bitcast_fusion.7
  160.3 1.0 fusion.88
  161.3 1.6 fusion.91
  163.1 1.6 fusion.90
  164.8 0.9 fusion.92
  165.8 0.7 constant_dynamic-update-slice_fusion.2
  166.5 28.0 %all-to-all-done.5 = bf16[64,2,80,128]{3,2,1,0:T(8,128)(2,1)S(1)} async-done(((bf16[64,2,80,128]{3,2,1,0:T(8,128)(2,1)}), bf16[64,2,80,128]{3,2,1,0:T(8,128)(2,1)S(1)}, u32[]{:S(2)}, u32[]{:S(2)}) %all-to-all-start.5) | async-done | bytes 2621472 | tf_op jit(solution)/shard_map/all_to_all | solution.py:160
  194.7 1.3 fusion.51
  196.1 2.4 convolution_add_fusion
  198.5 8.9 %all-to-all-start.4 = ((bf16[64,8,1024]{2,1,0:T(8,128)(2,1)}), bf16[64,8,1024]{2,1,0:T(8,128)(2,1)S(1)}, u32[]{:S(2)}, u32[]{:S(2)}) async-start(bf16[64,8,1024]{2,1,0:T(8,128)(2,1)} %bitcast.41), calls=%async_computation.4 | async-start | bytes 2097152 | tf_op jit(solution)/shard_map/all_to_all | solution.py:150
  207.6 0.7 fusion.56
  208.4 1.3 fusion.27
  209.7 1.3 fusion.29
  211.0 1.0 fusion.33
  212.0 1.0 fusion.34
  213.0 0.3 fusion.19
  213.3 20.8 %all-to-all-done.4 = bf16[64,8,1024]{2,1,0:T(8,128)(2,1)S(1)} async-done(((bf16[64,8,1024]{2,1,0:T(8,128)(2,1)}), bf16[64,8,1024]{2,1,0:T(8,128)(2,1)S(1)}, u32[]{:S(2)}, u32[]{:S(2)}) %all-to-all-start.4) | async-done | bytes 1048608 | tf_op jit(solution)/shard_map/all_to_all | solution.py:150
  234.1 0.6 gather_fusion
  234.7 0.9 fusion.35
  235.6 4.2 %reduce-scatter.2.cloned.1.call-done = f32[64,640]{1,0:T(8,128)} async-done(((f32[64,5120]{1,0:T(8,128)}), f32[64,640]{1,0:T(8,128)}) %reduce-scatter.2.cloned.1.call-update) | async-done | bytes 163856 | tf_op jit(solution)/shard_map/reduce_scatter | solution.py:163
  239.8 1.6 convert_element_type.80
  (52 shorter events, 2.2 us)
Async XLA Ops:
  7.2 21.2 %copy-start = (bf16[128,1024]{1,0:T(8,128)(2,1)S(1)}, bf16[128,1024]{1,0:T(8,128)(2,1)}, u32[]{:S(2)}) copy-start(bf16[128,1024]{1,0:T(8,128)(2,1)} %param.22) | copy-start | bytes 786436
  8.0 1.5 copy-start.7
  9.5 18.1 %copy-start.5 = (pred[16,8]{1,0:T(8,128)(4,1)}, pred[16,8]{1,0:T(8,128)(4,1)S(1)}, u32[]{:S(2)}) copy-start(pred[16,8]{1,0:T(8,128)(4,1)S(1)} %iota_compare_fusion.1) | copy-start | bytes 388
  11.2 16.4 %copy-start.2 = (bf16[128,1024]{1,0:T(8,128)(2,1)S(1)}, bf16[128,1024]{1,0:T(8,128)(2,1)}, u32[]{:S(2)}) copy-start(bf16[128,1024]{1,0:T(8,128)(2,1)} %param.25) | copy-start | bytes 786436
  13.5 25.6 %all-to-all-start.3 = ((f32[64,8,1,8]{3,1,2,0:T(8,128)}), f32[64,8,1,8]{3,1,2,0:T(8,128)}, u32[]{:S(2)}, u32[]{:S(2)}) async-start(f32[64,8,1,8]{3,1,2,0:T(8,128)} %get-tuple-element.164), calls=%async_computation.3 | async-start | bytes 524288 | tf_op jit(solution)/shard_map/all_to_all | solution.py:144
  39.1 18.1 %all-to-all-start.1 = ((f32[64,8,1,8]{3,1,2,0:T(8,128)}), f32[64,8,1,8]{3,1,2,0:T(8,128)}, u32[]{:S(2)}, u32[]{:S(2)}) async-start(f32[64,8,1,8]{3,1,2,0:T(8,128)} %get-tuple-element.165), calls=%async_computation.1 | async-start | bytes 524288 | tf_op jit(solution)/shard_map/all_to_all | solution.py:143
  90.2 8.3 %copy-start.10 = (bf16[80,128]{1,0:T(8,128)(2,1)S(1)}, bf16[80,128]{1,0:T(8,128)(2,1)}, u32[]{:S(2)}) copy-start(bf16[80,128]{1,0:T(8,128)(2,1)} %param.21) | copy-start | bytes 61444
  90.2 8.3 %copy-start.11 = (bf16[80,128]{1,0:T(8,128)(2,1)S(1)}, bf16[80,128]{1,0:T(8,128)(2,1)}, u32[]{:S(2)}) copy-start(bf16[80,128]{1,0:T(8,128)(2,1)} %param.20) | copy-start | bytes 61444
  90.2 34.9 %all-to-all-start = ((bf16[64,8,1024]{2,1,0:T(8,128)(2,1)}), bf16[64,8,1024]{2,1,0:T(8,128)(2,1)S(1)}, u32[]{:S(2)}, u32[]{:S(2)}) async-start(bf16[64,8,1024]{2,1,0:T(8,128)(2,1)} %get-tuple-element.167), calls=%async_computation | async-start | bytes 2097152 | tf_op jit(solution)/shard_map/all_to_all | solution.py:139
  125.1 1.9 copy-start.1
  127.0 8.3 %copy-start.4 = (bf16[64,128]{1,0:T(8,128)(2,1)S(1)}, bf16[64,128]{1,0:T(8,128)(2,1)}, u32[]{:S(2)}) copy-start(bf16[64,128]{1,0:T(8,128)(2,1)} %param.19) | copy-start | bytes 49156
  127.0 67.6 %all-to-all-start.5 = ((bf16[64,2,80,128]{3,2,1,0:T(8,128)(2,1)}), bf16[64,2,80,128]{3,2,1,0:T(8,128)(2,1)S(1)}, u32[]{:S(2)}, u32[]{:S(2)}) async-start(bf16[64,2,80,128]{3,2,1,0:T(8,128)(2,1)} %stack.11), calls=%async_computation.5 | async-start | bytes 5242880 | tf_op jit(solution)/shard_map/all_to_all | solution.py:160
  135.2 104.6 %reduce-scatter.2.cloned.1.call-start = ((), (), s32[]{:S(2)}) async-start(), calls=%async_computation.7 | async-start | bytes 1474560 | tf_op jit(solution)/shard_map/reduce_scatter | solution.py:163
  198.5 9.0 %copy-start.12 = (pred[16]{0:T(512)(128)(4,1)S(1)}, pred[16]{0:T(512)(128)(4,1)}, u32[]{:S(2)}) copy-start(pred[16]{0:T(512)(128)(4,1)} %get-tuple-element.156) | copy-start | bytes 52
  198.5 9.9 %copy-start.9 = (bf16[128,128]{1,0:T(8,128)(2,1)S(1)}, bf16[128,128]{1,0:T(8,128)(2,1)}, u32[]{:S(2)}) copy-start(bf16[128,128]{1,0:T(8,128)(2,1)} %param.23) | copy-start | bytes 98308
  198.5 11.1 %copy-start.3 = (bf16[128,1024]{1,0:T(8,128)(2,1)S(1)}, bf16[128,1024]{1,0:T(8,128)(2,1)}, u32[]{:S(2)}) copy-start(bf16[128,1024]{1,0:T(8,128)(2,1)} %param.25) | copy-start | bytes 786436
  198.5 11.1 %copy-start.6 = (pred[16,8]{1,0:T(8,128)(4,1)S(1)}, pred[16,8]{1,0:T(8,128)(4,1)}, u32[]{:S(2)}) copy-start(pred[16,8]{1,0:T(8,128)(4,1)} %copy-done.5) | copy-start | bytes 388
  198.5 11.1 %copy-start.8 = (bf16[128,128]{1,0:T(8,128)(2,1)S(1)}, bf16[128,128]{1,0:T(8,128)(2,1)}, u32[]{:S(2)}) copy-start(bf16[128,128]{1,0:T(8,128)(2,1)} %param.24) | copy-start | bytes 98308
  198.5 35.6 %all-to-all-start.4 = ((bf16[64,8,1024]{2,1,0:T(8,128)(2,1)}), bf16[64,8,1024]{2,1,0:T(8,128)(2,1)S(1)}, u32[]{:S(2)}, u32[]{:S(2)}) async-start(bf16[64,8,1024]{2,1,0:T(8,128)(2,1)} %bitcast.41), calls=%async_computation.4 | async-start | bytes 2097152 | tf_op jit(solution)/shard_map/all_to_all | solution.py:150
Sparse Core Ops, SparseCore 0:
  198.6 41.1 reduce-scatter.1
